TPU v7x, 256 devices: a whole 4x4x8 slice. The times are simulated.
256 devices in a mesh: ctx: 64 (over y, z_lo, x), head: 4 (over z_hi, core).
Axes of the slice: x: 4, y: 4, z: 8 (z_hi: 2, z_lo: 4; z = z_hi * 4 + z_lo), core: 2. Of those that a mesh axis runs over, the one named last changes fastest.
Arguments:
- queries: bfloat16 [16384, 8192], P('ctx', 'head'), may hold values from -1.78125 to 1.78125
- key_rows: bfloat16 [16384, 8192], P('ctx', 'head'), may hold values from -1.78125 to 1.78125
- value_rows: bfloat16 [16384, 8192], P('ctx', 'head'), may hold values from -18 to 18
- cotangent: bfloat16 [16384, 8192], P('ctx', 'head'), may hold values from -6 to 6
- log_decay: float32 [64, 16384], P('head', 'ctx'), may hold values from -0.6 to 0, as said below
- norm_gain: float32 [8192], P('head'), may hold values from 0.25 to 1.75
Outputs:
- grad_queries: bfloat16 [16384, 8192], P('ctx', 'head')
- grad_keys: bfloat16 [16384, 8192], P('ctx', 'head')
- grad_values: bfloat16 [16384, 8192], P('ctx', 'head')
Inputs may be any that keep to these rules, and one draw needn't show every extreme that they name: `log_decay`: per-position logarithm of each head's decay.
All inputs are finite; a program needn't handle non-finite values.
Results may differ from a plain program's by a relative error of at most 0.007.
Values sent between devices are 32-bit elements; how exact they have to be, the bound alone decides.
A program may use at most 320 MiB of HBM per device.

v0:
```python
import jax
import jax.numpy as jnp
from jax import lax
from jax.sharding import PartitionSpec as P

eps_norm = 1e-06


def carried_in(value, axis, join, neutral, backward):
    count, mine = (lax.axis_size(axis), lax.axis_index(axis))
    pieces = jax.tree.map(lambda part: lax.all_gather(part, axis), value)
    if backward:
        pieces = jax.tree.map(lambda part: part[::-1], pieces)
        mine = count - 1 - mine
    running = jax.tree.map(
        lambda part, zero: jnp.full_like(part, 0) + jnp.asarray(zero, part.dtype), value, neutral
    )

    def lap(position, running):
        longer = join(running, jax.tree.map(lambda part: part[position], pieces))
        return jax.tree.map(lambda new, old: jnp.where(position < mine, new, old), longer, running)

    return lax.fori_loop(0, count - 1, lap, running)


def link_states(earlier, later):
    return (earlier[0] * later[0], later[0][:, None, None] * earlier[1] + later[1])


def causal_decay(cumulative):
    row_count = cumulative.shape[1]
    row_index = lax.broadcasted_iota(jnp.int32, (row_count, row_count), 0)
    col_index = lax.broadcasted_iota(jnp.int32, (row_count, row_count), 1)
    lower_mask = (row_index >= col_index)[None]
    spread = cumulative[:, :, None] - cumulative[:, None, :]
    return jnp.where(lower_mask, jnp.exp(jnp.minimum(spread, 0.0)), 0.0)


def product(pattern, left_side, right_side):
    return jnp.einsum(pattern, left_side, right_side, preferred_element_type=jnp.float32)


def whole_prefix(fall, block_state):
    start_pair = (jnp.ones_like(fall), jnp.zeros_like(block_state))
    return carried_in((fall, block_state), "ctx", link_states, start_pair, False)[1]


def whole_suffix(fall, block_grad):
    start_pair = (jnp.ones_like(fall), jnp.zeros_like(block_grad))
    return carried_in((fall, block_grad), "ctx", link_states, start_pair, True)[1]


def shards(queries, key_rows, value_rows, cotangent, log_decay, norm_gain):
    row_count = queries.shape[0]
    head_count = log_decay.shape[0]
    head_width = queries.shape[1] // head_count
    features = lax.axis_size("head") * queries.shape[1]
    query_heads = queries.reshape(row_count, head_count, head_width)
    key_heads = key_rows.reshape(row_count, head_count, head_width)
    value_heads = value_rows.reshape(row_count, head_count, head_width)
    cumulative = jnp.cumsum(log_decay, axis=1)
    ending = cumulative[:, -1:]
    fall = jnp.exp(cumulative[:, -1])
    forward_gain = jnp.exp(cumulative).T[:, :, None]
    backward_gain = jnp.exp(ending - cumulative).T[:, :, None]
    key_weight = (key_heads * backward_gain).astype(jnp.bfloat16)
    query_weight = (query_heads * forward_gain).astype(jnp.bfloat16)
    value_weight = (value_heads * backward_gain).astype(jnp.bfloat16)
    block_state = product("thd,the->hde", key_weight, value_heads)
    entry_state = whole_prefix(fall, block_state)
    entry_low = entry_state.astype(jnp.bfloat16)
    decay_mask = causal_decay(cumulative)
    scores_fwd = (product("thd,jhd->htj", query_heads, key_heads) * decay_mask).astype(jnp.bfloat16)
    output_f = product("htj,jhe->the", scores_fwd, value_heads) + product(
        "thd,hde->the", query_weight, entry_low
    )
    flat_out = output_f.reshape(row_count, -1)
    scaled = norm_gain * cotangent
    square_sum, inner_sum = lax.psum(
        (jnp.sum(flat_out * flat_out, axis=1), jnp.sum(flat_out * scaled, axis=1)), "head"
    )
    root_mean = jnp.sqrt(square_sum / features + eps_norm)
    d_out = (
        scaled / root_mean[:, None] - flat_out * (inner_sum / (features * root_mean**3))[:, None]
    ).astype(jnp.bfloat16)
    d_out_heads = d_out.reshape(row_count, head_count, head_width)
    back_scores = (product("thd,jhd->htj", d_out_heads, value_heads) * decay_mask).astype(
        jnp.bfloat16
    )
    dout_weight = (d_out_heads * forward_gain).astype(jnp.bfloat16)
    grad_q = product("htj,jhd->thd", back_scores, key_heads) + product(
        "the,hde->thd", dout_weight, entry_low
    )
    block_grad = product("thd,the->hde", query_weight, d_out_heads)
    exit_state = whole_suffix(fall, block_grad)
    exit_low = exit_state.astype(jnp.bfloat16)
    grad_k = product("hjt,jhd->thd", back_scores, query_heads) + product(
        "the,hde->thd", value_weight, exit_low
    )
    grad_v = product("hjt,jhe->the", scores_fwd, d_out_heads) + product(
        "thd,hde->the", key_weight, exit_low
    )
    out_shape = (row_count, head_count * head_width)
    return (
        grad_q.reshape(out_shape).astype(jnp.bfloat16),
        grad_k.reshape(out_shape).astype(jnp.bfloat16),
        grad_v.reshape(out_shape).astype(jnp.bfloat16),
    )


def solution(mesh):
    in_specs = (
        P("ctx", "head"),
        P("ctx", "head"),
        P("ctx", "head"),
        P("ctx", "head"),
        P("head", "ctx"),
        P("head"),
    )
    out_specs = (P("ctx", "head"), P("ctx", "head"), P("ctx", "head"))
    return jax.shard_map(shards, mesh=mesh, in_specs=in_specs, out_specs=out_specs, check_vma=False)
```

profile of v0, /device:TPU:8, one launch (start us, length us, event | category | flops | bytes accessed | tf_op | source)
XLA Modules:
  0.0 1750.2 jit_solution(17206473319592139192)
XLA Ops:
  9.2 3.6 fusion.8
  14.3 170.2 %all-reduce = f32[1024]{0:T(1024)S(1)} all-reduce(f32[1024]{0:T(1024)S(1)} %dynamic-update-slice), channel_id=2, replica_groups=mesh['ctx'=64,'head'=4] {'ctx'}, use_global_device_ids=true, to_apply=%add | all-reduce | flops 1024 | bytes 8192
  184.6 1.5 copy.121
  186.1 1.6 multiply_convert_fusion.1
  189.0 2.2 fusion.4
  191.2 555.2 %all-gather.6.cloned.1.call-done = f32[1024,128,128]{2,1,0:T(8,128)} async-done(((f32[16,128,128]{2,1,0:T(8,128)}), f32[1024,128,128]{2,1,0:T(8,128)}) %all-gather.6.cloned.1.call-update) | async-done | bytes 67108880 | tf_op jit(solution)/shard_map/all_gather | solution.py:11
  746.3 94.4 %while.28 = (s32[]{:T(128)}, f32[16,128,128]{2,1,0:T(8,128)S(1)}, s32[]{:T(128)}, f32[64,16]{1,0:T(8,128)S(1)}, f32[64,16,128,128]{3,2,1,0:T(8,128)}, /*index=5*/s32[]{:T(128)}, s32[]{:T(128)}) while((s32[]{:T(128)}, f32[16,128,128]{2,1,0:T(8,128)S(1)}, s32[]{:T(128)}, f32[64,16]{1,0:T(8,128)S(1)}, f32[64,16,128,128]{3,2,1,0:T(8,128)}, ...), condition=%wide.region_3.4_spmd.clone, body=%wide.region_2.3_spmd.clone.sunk | while | flops 1048580 | bytes 3146025 | solution.py:23
  840.8 3.5 multiply_reduce_fusion.1
  844.2 3.0 copy.102
  847.3 1.9 multiply_reduce_fusion
  849.2 12.6 all-reduce.1
  861.8 3.0 subtract_convert_fusion
  866.3 3.1 fusion.15
  869.5 2.9 multiply_convert_fusion
  875.9 2.4 copy.113
  878.2 3.5 fusion.30
  881.8 1.7 fusion.31
  883.5 710.6 %all-gather.8.cloned.1.call-done = f32[1024,128,128]{2,1,0:T(8,128)} async-done(((f32[16,128,128]{2,1,0:T(8,128)}), f32[1024,128,128]{2,1,0:T(8,128)}) %all-gather.8.cloned.1.call-update) | async-done | bytes 67108880 | tf_op jit(solution)/shard_map/all_gather | solution.py:11
  1594.1 43.8 %rev.7 = f32[64,16,128,128]{3,2,1,0:T(8,128)} reverse(f32[64,16,128,128]{3,2,1,0:T(8,128)} %bitcast.11), dimensions={0} | reverse | bytes 134217728 | tf_op jit(solution)/shard_map/rev | solution.py:13
  1637.9 94.4 %while.29 = (s32[]{:T(128)}, f32[16,128,128]{2,1,0:T(8,128)S(1)}, s32[]{:T(128)}, f32[64,16]{1,0:T(8,128)S(1)}, f32[64,16,128,128]{3,2,1,0:T(8,128)}, /*index=5*/s32[]{:T(128)}, s32[]{:T(128)}) while((s32[]{:T(128)}, f32[16,128,128]{2,1,0:T(8,128)S(1)}, s32[]{:T(128)}, f32[64,16]{1,0:T(8,128)S(1)}, ...), condition=%wide.region_9.10_spmd.clone, body=%wide.region_8.9_spmd.clone.sunk | while | flops 1048580 | bytes 3146025 | solution.py:23
  1732.4 3.2 add_convert_fusion
  1735.6 2.4 copy.115
  1738.0 3.2 fusion.2
  1741.1 2.3 copy.114
  (304 shorter events, 194.2 us)
Async XLA Ops:
  7.2 2.0 copy-start
  7.2 739.2 %all-gather.6.cloned.1.call-start = ((), (), s32[]{:S(2)}) async-start(), calls=%async_computation | async-start | bytes 68157440 | tf_op jit(solution)/shard_map/all_gather | solution.py:11
  9.2 3.7 copy-start.13
  12.8 1581.4 %all-gather.8.cloned.1.call-start = ((), (), s32[]{:S(2)}) async-start(), calls=%async_computation.1 | async-start | bytes 68157440 | tf_op jit(solution)/shard_map/all_gather | solution.py:11
  186.1 654.7 %copy-start.4 = (bf16[256,2048]{0,1:T(8,128)(2,1)}, bf16[256,2048]{0,1:T(8,128)(2,1)S(1)}, u32[]{:S(2)}) copy-start(bf16[256,2048]{0,1:T(8,128)(2,1)S(1)} %copy.121) | copy-start | bytes 3145732
  186.1 2.9 copy-start.9
  187.7 1.3 copy-start.6
  844.2 3.0 copy-start.11
  844.2 3.0 copy-start.12
  866.3 3.1 copy-start.1
  872.4 1.3 copy-start.7
  872.4 2.0 copy-start.2
  875.9 2.4 copy-start.3
  878.2 3.5 copy-start.5
  878.2 3.5 copy-start.8
  1735.6 2.4 copy-start.10
Sparse Core Ops, SparseCore 0:
  12.9 733.4 all-gather.5
  869.5 724.5 all-gather.7
where the time goes:
time: 1760 us; the launch traced here: 1750 us
  waiting for transfers between devices  1270 us (72%)
  other arithmetic  189 us (11%)
  blocking collectives  183 us (10%)
  local copies, waits for them, and re-layouts  62.5 us (4%)
  matrix products  30.7 us (2%)
    all_gather x2, waiting for transfers between devices, carried_in(): pieces = jax.tree.map(lambda part: lax.all_gather(part, axis), value)  1270 us
    select_n x126, other arithmetic, lap(): jnp.where(position < mine, new, old)  184 us
    unnamed x1, blocking collectives  170 us
    rev x2, local copies, waits for them, and re-layouts, carried_in(): pieces = jax.tree.map(lambda part: part[::-1], pieces)  43.8 us
  transfers between devices with their start and end apart: 2, of which 2 were waited for; matrix products, arithmetic and copies ran while one was open for 1% of the time, Pallas kernels for 0%

commit v1 on v0

v1 whole, which is shorter than its diff:
```python
import functools
import itertools

import jax
import jax.numpy as jnp
from jax import lax
from jax.experimental import pallas as pl
from jax.experimental.pallas import tpu as pltpu
from jax.sharding import PartitionSpec as P

eps_norm = 1e-06
MESH = pl.DeviceIdType.MESH
F32, BF16 = jnp.float32, jnp.bfloat16
DH = 128
PARTS = {64: (4, 4, 4), 8: (2, 2, 2)}
X_OUT, Z_OUT, Y_ALL, Z_BACK, X_BACK = range(5)


def nn(a, b, **kw):
    return lax.dot_general(a, b, (((1,), (0,)), ((), ())), preferred_element_type=F32, **kw)


def nt(a, b, **kw):
    return lax.dot_general(a, b, (((1,), (1,)), ((), ())), preferred_element_type=F32, **kw)


def tn(a, b, **kw):
    return lax.dot_general(a, b, (((0,), (0,)), ((), ())), preferred_element_type=F32, **kw)


def kernel(
    dims, q_ref, k_ref, v_ref, cot_ref, ld_ref, gain_ref, gq_ref, gk_ref, gv_ref,
    cc, crow, kw, vw, qw, mask, sc, of, dob, gkf, gvf, stat,
    st, xr, tz, zr, uy, yr, ez, er, ex, fin,
    xds, xd, zds, zd, yds, yd, hs, hr,
    send_sem, recv_sem, dsend, drecv, hsend, hrecv,
):
    ny, nz, nx, nhd, chunks = dims
    rows = q_ref.shape[0]
    half = rows // 2
    heads = ld_ref.shape[0]
    piece = heads // nx
    nh = piece // chunks
    zr_rows = DH // nz
    exact = dict(precision=lax.Precision.HIGHEST)

    me = lax.axis_index("ctx")
    hd = lax.axis_index("head")
    x = lax.rem(me, nx)
    z = lax.rem(lax.div(me, nx), nz)
    y = lax.div(me, nx * nz)

    def x_at(i):
        return lax.rem(x + i, nx)

    def z_at(i):
        return lax.rem(z + i, nz)

    def y_at(i):
        return lax.rem(y + i, ny)

    def x_dev(i):
        return {"ctx": me - x + x_at(i), "head": hd}

    def z_dev(i):
        return {"ctx": me + (z_at(i) - z) * nx, "head": hd}

    def y_dev(i):
        return {"ctx": me + (y_at(i) - y) * (nx * nz), "head": hd}

    def h_dev(i):
        return {"ctx": me, "head": lax.rem(hd + i, nhd)}

    partners = (
        [x_dev(i) for i in range(1, nx)] + [z_dev(i) for i in range(1, nz)]
        + [y_dev(i) for i in range(1, ny)] + [h_dev(i) for i in range(1, nhd)]
    )
    barrier = pltpu.get_barrier_semaphore()
    for device in partners:
        pl.semaphore_signal(barrier, inc=1, device_id=device, device_id_type=MESH)

    copies = []

    def push(src, dst, send, recv, device):
        copy = pltpu.make_async_remote_copy(
            src_ref=src, dst_ref=dst, send_sem=send, recv_sem=recv, device_id=device, device_id_type=MESH
        )
        copy.start()
        copies.append(copy)
        return copy

    def columns(h):
        if isinstance(h, int):
            return pl.ds(h * DH, DH)
        return pl.ds(pl.multiple_of(h * DH, DH), DH)

    def order(count):
        return sorted(range(1, count), key=lambda i: -min(i, count - i))

    ld = ld_ref[...]
    r_i = lax.broadcasted_iota(jnp.int32, (rows, rows), 0)
    c_i = lax.broadcasted_iota(jnp.int32, (rows, rows), 1)
    crow[...] = nn(ld, (r_i <= c_i).astype(F32), **exact)
    cum_t = nt((r_i >= c_i).astype(F32), ld, **exact)
    end_t = cum_t[rows - 1:rows, :]
    bg_t = jnp.exp(end_t - cum_t)
    fall_t = jnp.exp(end_t)
    for h in range(heads):
        cc[h] = jnp.broadcast_to(cum_t[:, h:h + 1], (rows, DH))
        xds[h // piece, h % piece] = jnp.broadcast_to(fall_t[:, h:h + 1], (8, DH))

    pl.semaphore_wait(barrier, len(partners))

    xd_copies = [
        push(xds.at[x_at(i)], xd.at[x], dsend.at[0, i - 1], drecv.at[0, i - 1], x_dev(i)) for i in order(nx)
    ]
    xd[x] = xds[x]

    pending = {}

    def x_send(way, c):
        for i in order(nx):
            pending[way, X_OUT, c, i] = push(
                st.at[way, c, x_at(i)], xr.at[way, c, x],
                send_sem.at[way, X_OUT, c, i - 1], recv_sem.at[way, X_OUT, c, i - 1], x_dev(i),
            )
        xr[way, c, x] = st[way, c, x]

    def arrive(way, level, c, count):
        for i in order(count):
            pending[way, level, c, i].wait_recv()

    def along(way, count):
        return range(count) if way == 0 else range(count - 1, -1, -1)

    def head_of(c, p, n):
        return p * piece + c * nh + n

    for c in range(chunks):
        for p in range(nx):
            for n in range(nh):
                h = head_of(c, p, n)
                back = jnp.broadcast_to(bg_t[:, h:h + 1], (rows, DH))
                weighted = (k_ref[:, columns(h)].astype(F32) * back).astype(BF16)
                kw[:, columns(h)] = weighted
                st[0, c, p, n] = tn(weighted, v_ref[:, columns(h)])
        x_send(0, c)

    def z_decays():
        for copy in xd_copies:
            copy.wait_recv()
        total = xd[0]
        for s in range(1, nx):
            total = total * xd[s]
        zds[...] = total
        zd[z] = total
        return [push(zds, zd.at[z], dsend.at[1, i - 1], drecv.at[1, i - 1], z_dev(i)) for i in order(nz)]

    def y_decays(zd_copies):
        for copy in zd_copies:
            copy.wait_recv()
        total = zd[0]
        for s in range(1, nz):
            total = total * zd[s]
        yds[...] = total
        yd[y] = total
        return [push(yds, yd.at[y], dsend.at[2, i - 1], drecv.at[2, i - 1], y_dev(i)) for i in order(ny)]

    def x_reduce(way, c):
        arrive(way, X_OUT, c, nx)
        for n in range(nh):
            path = list(along(way, nx))
            total = xr[way, c, path[0], n]
            for s in path[1:]:
                total = xd[s, c * nh + n, 0:1, :] * total + xr[way, c, s, n]
            tz[way, c, n] = total
        for i in order(nz):
            pending[way, Z_OUT, c, i] = push(
                tz.at[way, c, :, pl.ds(z_at(i) * zr_rows, zr_rows), :], zr.at[way, c, z],
                send_sem.at[way, Z_OUT, c, i - 1], recv_sem.at[way, Z_OUT, c, i - 1], z_dev(i),
            )
        zr[way, c, z] = tz[way, c, :, pl.ds(z * zr_rows, zr_rows), :]

    def z_reduce(way, c):
        arrive(way, Z_OUT, c, nz)
        for n in range(nh):
            path = list(along(way, nz))
            total = zr[way, c, path[0], n]
            for s in path[1:]:
                total = zd[s, c * nh + n, 0:1, :] * total + zr[way, c, s, n]
            uy[way, c, n] = total
        for i in order(ny):
            pending[way, Y_ALL, c, i] = push(
                uy.at[way, c], yr.at[way, c, y],
                send_sem.at[way, Y_ALL, c, i - 1], recv_sem.at[way, Y_ALL, c, i - 1], y_dev(i),
            )
        yr[way, c, y] = uy[way, c]

    def z_expand(way, c):
        arrive(way, Y_ALL, c, ny)
        for n in range(nh):
            state = jnp.zeros((zr_rows, DH), F32)
            for s in along(way, ny):
                longer = yd[s, c * nh + n, 0:1, :] * state + yr[way, c, s, n]
                before = (s < y) if way == 0 else (s > y)
                state = jnp.where(before, longer, state)
            for s in along(way, nz):
                ez[way, c, s, n] = state
                state = zd[s, c * nh + n, 0:1, :] * state + zr[way, c, s, n]
        for i in order(nz):
            pending[way, Z_BACK, c, i] = push(
                ez.at[way, c, z_at(i)], er.at[way, c, :, pl.ds(z * zr_rows, zr_rows), :],
                send_sem.at[way, Z_BACK, c, i - 1], recv_sem.at[way, Z_BACK, c, i - 1], z_dev(i),
            )
        er[way, c, :, pl.ds(z * zr_rows, zr_rows), :] = ez[way, c, z]

    def x_expand(way, c):
        arrive(way, Z_BACK, c, nz)
        for n in range(nh):
            state = er[way, c, n]
            for s in along(way, nx):
                ex[way, c, s, n] = state
                state = xd[s, c * nh + n, 0:1, :] * state + xr[way, c, s, n]
        for i in order(nx):
            pending[way, X_BACK, c, i] = push(
                ex.at[way, c, x_at(i)], fin.at[way, c, x],
                send_sem.at[way, X_BACK, c, i - 1], recv_sem.at[way, X_BACK, c, i - 1], x_dev(i),
            )
        fin[way, c, x] = ex[way, c, x]

    def loop(count, body):
        pair = 2 if count % 2 == 0 else 1

        def step(j, carry):
            for u in range(pair):
                body(j * pair + u)
            return carry

        lax.fori_loop(0, count // pair, step, 0)

    lower = (
        lax.broadcasted_iota(jnp.int32, (half, half), 0) >= lax.broadcasted_iota(jnp.int32, (half, half), 1)
    )

    def forward_work(h):
        here = columns(h)
        col = cc[h]
        line = crow[pl.ds(h, 1), :]
        m00 = jnp.where(lower, jnp.exp(jnp.minimum(col[:half] - line[:, :half], 0.0)), 0.0)
        m10 = jnp.exp(jnp.minimum(col[half:] - line[:, :half], 0.0))
        m11 = jnp.where(lower, jnp.exp(jnp.minimum(col[half:] - line[:, half:], 0.0)), 0.0)
        mask[h, 0], mask[h, 1], mask[h, 2] = m00, m10, m11
        q, k, v = q_ref[:, here], k_ref[:, here], v_ref[:, here]
        top = (nt(q[:half], k[:half]) * m00).astype(BF16)
        bottom = nt(q[half:], k)
        low_left = (bottom[:, :half] * m10).astype(BF16)
        low_right = (bottom[:, half:] * m11).astype(BF16)
        sc[h, 0], sc[h, 1], sc[h, 2] = top, low_left, low_right
        of[:half, here] = nn(top, v[:half])
        of[half:, here] = nn(low_left, v[:half]) + nn(low_right, v[half:])
        qw[:, here] = (q.astype(F32) * jnp.exp(col)).astype(BF16)
        vw[:, here] = (v.astype(F32) * jnp.exp(col[rows - 1:rows, :] - col)).astype(BF16)

    def enter(c):
        arrive(0, X_BACK, c, nx)

        def one(j):
            p, n = lax.div(j, nh), lax.rem(j, nh)
            here = columns(head_of(c, p, n))
            out = of[:, here] + nn(qw[:, here], fin[0, c, p, n].astype(BF16))
            of[:, here] = out
            scaled = gain_ref[:, here] * cot_ref[:, here].astype(F32)
            stat[0] += out * out
            stat[1] += out * scaled

        loop(nx * nh, one)

    def backward_work(c):
        def one(j):
            p, n = lax.div(j, nh), lax.rem(j, nh)
            h = head_of(c, p, n)
            here = columns(h)
            d_out = dob[:, here]
            q, k, v = q_ref[:, here], k_ref[:, here], v_ref[:, here]
            top = (nt(d_out[:half], v[:half]) * mask[h, 0]).astype(BF16)
            bottom = nt(d_out[half:], v)
            low_left = (bottom[:, :half] * mask[h, 1]).astype(BF16)
            low_right = (bottom[:, half:] * mask[h, 2]).astype(BF16)
            entry = fin[0, c, p, n].astype(BF16)
            weighted = (d_out.astype(F32) * jnp.exp(cc[h])).astype(BF16)
            cross = nt(weighted, entry)
            gq_ref[:half, here] = (nn(top, k[:half]) + cross[:half]).astype(BF16)
            gq_ref[half:, here] = (nn(low_left, k[:half]) + nn(low_right, k[half:]) + cross[half:]).astype(BF16)
            gkf[:half, here] = tn(top, q[:half]) + tn(low_left, q[half:])
            gkf[half:, here] = tn(low_right, q[half:])
            gvf[:half, here] = tn(sc[h, 0], d_out[:half]) + tn(sc[h, 1], d_out[half:])
            gvf[half:, here] = tn(sc[h, 2], d_out[half:])

        loop(nx * nh, one)

    def leave(c):
        arrive(1, X_BACK, c, nx)

        def one(j):
            p, n = lax.div(j, nh), lax.rem(j, nh)
            here = columns(head_of(c, p, n))
            low = fin[1, c, p, n].astype(BF16)
            gk_ref[:, here] = (gkf[:, here] + nt(vw[:, here], low)).astype(BF16)
            gv_ref[:, here] = (gvf[:, here] + nn(kw[:, here], low)).astype(BF16)

        loop(nx * nh, one)

    def scan(way, tasks, last):
        tasks = iter(tasks)
        levels = [x_reduce, z_reduce, z_expand, x_expand]

        def fill(count):
            for task in itertools.islice(tasks, count):
                task()

        for step in range(chunks + len(levels)):
            for lag in range(len(levels), -1, -1):
                c = step - lag
                if 0 <= c < chunks:
                    if lag == len(levels):
                        fill(None)
                        last(c)
                    else:
                        levels[lag](way, c)
            fill(1)
        fill(None)

    group = max(heads // chunks, 1)

    def forward_group(g):
        loop(group, lambda j: forward_work(g * group + j))

    stat[...] = jnp.zeros_like(stat)
    zd_copies = z_decays()
    forward_group(0)
    yd_copies = y_decays(zd_copies)
    if chunks > 1:
        forward_group(1)
    for copy in yd_copies:
        copy.wait_recv()
    scan(0, [functools.partial(forward_group, g) for g in range(2, chunks)], enter)

    ones = jnp.ones((8, DH), F32)
    pick = lax.broadcasted_iota(jnp.int32, (8, rows), 0) < 4
    hs[...] = jnp.where(pick, nt(ones, stat[0], **exact), nt(ones, stat[1], **exact))
    hr[hd] = hs[...]
    h_copies = [push(hs, hr.at[hd], hsend.at[i - 1], hrecv.at[i - 1], h_dev(i)) for i in order(nhd)]
    for copy in h_copies:
        copy.wait_recv()
    both = hr[0]
    for s in range(1, nhd):
        both = both + hr[s]
    features = nhd * q_ref.shape[1]
    where = lax.broadcasted_iota(jnp.int32, (8, DH), 0)
    square_sum = tn(both, (where == 0).astype(F32), **exact)
    inner_sum = tn(both, (where == 4).astype(F32), **exact)
    root_mean = jnp.sqrt(square_sum / features + eps_norm)
    stat[0] = 1.0 / root_mean
    stat[1] = inner_sum / (features * root_mean * root_mean * root_mean)

    for c in range(chunks):
        def one(j, c=c):
            p, n = lax.div(j, nh), lax.rem(j, nh)
            here = columns(head_of(c, p, n))
            scaled = gain_ref[:, here] * cot_ref[:, here].astype(F32)
            d_out = (scaled * stat[0] - of[:, here] * stat[1]).astype(BF16)
            dob[:, here] = d_out
            st[1, c, p, n] = tn(qw[:, here], d_out)

        loop(nx * nh, one)
        x_send(1, c)

    backward_work(0)
    scan(1, [functools.partial(backward_work, c) for c in range(1, chunks)], leave)

    for copy in copies:
        copy.wait_send()


def shards(dims, queries, key_rows, value_rows, cotangent, log_decay, norm_gain):
    ny, nz, nx, nhd, chunks = dims
    rows, width = queries.shape
    heads = log_decay.shape[0]
    piece = heads // nx
    nh = piece // chunks
    zrows = DH // nz
    half = rows // 2
    vmem = pltpu.VMEM
    dma = pltpu.SemaphoreType.DMA
    most = max(nx, ny, nz) - 1
    scratch = [
        vmem((heads, rows, DH), F32),
        vmem((heads, rows), F32),
        vmem((rows, width), BF16),
        vmem((rows, width), BF16),
        vmem((rows, width), BF16),
        vmem((heads, 3, half, half), F32),
        vmem((heads, 3, half, half), BF16),
        vmem((rows, width), F32),
        vmem((rows, width), BF16),
        vmem((rows, width), F32),
        vmem((rows, width), F32),
        vmem((2, rows, DH), F32),
        vmem((2, chunks, nx, nh, DH, DH), F32),
        vmem((2, chunks, nx, nh, DH, DH), F32),
        vmem((2, chunks, nh, DH, DH), F32),
        vmem((2, chunks, nz, nh, zrows, DH), F32),
        vmem((2, chunks, nh, zrows, DH), F32),
        vmem((2, chunks, ny, nh, zrows, DH), F32),
        vmem((2, chunks, nz, nh, zrows, DH), F32),
        vmem((2, chunks, nh, DH, DH), F32),
        vmem((2, chunks, nx, nh, DH, DH), F32),
        vmem((2, chunks, nx, nh, DH, DH), F32),
        vmem((nx, piece, 8, DH), F32),
        vmem((nx, piece, 8, DH), F32),
        vmem((piece, 8, DH), F32),
        vmem((nz, piece, 8, DH), F32),
        vmem((piece, 8, DH), F32),
        vmem((ny, piece, 8, DH), F32),
        vmem((8, rows), F32),
        vmem((nhd, 8, rows), F32),
        dma((2, 5, chunks, most)),
        dma((2, 5, chunks, most)),
        dma((3, most)),
        dma((3, most)),
        dma((max(nhd - 1, 1),)),
        dma((max(nhd - 1, 1),)),
    ]
    return pl.pallas_call(
        functools.partial(kernel, dims),
        out_shape=[jax.ShapeDtypeStruct((rows, width), BF16)] * 3,
        in_specs=[pl.BlockSpec(memory_space=pltpu.VMEM)] * 6,
        out_specs=[pl.BlockSpec(memory_space=pltpu.VMEM)] * 3,
        scratch_shapes=scratch,
        compiler_params=pltpu.CompilerParams(
            collective_id=0, has_side_effects=True, vmem_limit_bytes=56 * 1024 * 1024
        ),
    )(queries, key_rows, value_rows, cotangent, log_decay, norm_gain.reshape(1, width))


def solution(mesh):
    ny, nz, nx = PARTS[mesh.shape["ctx"]]
    dims = (ny, nz, nx, mesh.shape["head"], 4 if mesh.shape["ctx"] == 64 else 2)
    in_specs = (
        P("ctx", "head"),
        P("ctx", "head"),
        P("ctx", "head"),
        P("ctx", "head"),
        P("head", "ctx"),
        P("head"),
    )
    out_specs = (P("ctx", "head"), P("ctx", "head"), P("ctx", "head"))
    return jax.shard_map(
        functools.partial(shards, dims), mesh=mesh, in_specs=in_specs, out_specs=out_specs, check_vma=False
    )
```

time: 1760 us -> 109 us (0.06)
  waiting for transfers between devices: 1270 us -> 0 us
  other arithmetic: 189 us -> 0 us
  blocking collectives: 183 us -> 0 us
  Pallas kernels: 0 us -> 104 us
  local copies, waits for them, and re-layouts: 62.5 us -> 4.97 us
  matrix products: 30.7 us -> 0 us
    all_gather x2 -> x0, waiting for transfers between devices: 1270 us -> none  [carried_in(): pieces = jax.tree.map(lambda part: lax.all_gather(part, axis), value)]
    select_n x126 -> x0, other arithmetic: 184 us -> none  [lap(): jnp.where(position < mine, new, old)]
    unnamed x1 -> x0, blocking collectives: 170 us -> none
    pallas_call x0 -> x1, Pallas kernels: none -> 104 us  [shards(): pl.pallas_call(functools.partial(kernel, dims), out_shape=[jax.ShapeDtype...]
    rev x2 -> x0, local copies, waits for them, and re-layouts: 43.8 us -> none  [carried_in(): pieces = jax.tree.map(lambda part: part[::-1], pieces)]
    dot_general x12 -> x0, matrix products: 30.7 us -> none  [product(): jnp.einsum(pattern, left_side, right_side, preferred_element_type=jnp.flo...]
  transfers between devices with their start and end apart: 2 -> 0, of which waited for: 2 -> 0; matrix products, arithmetic and copies ran while one was open for 1% -> 0% of each run, Pallas kernels for 0% -> 0%
where the time goes in v1:
time: 109 us
  Pallas kernels  104 us (95%)
  local copies, waits for them, and re-layouts  4.97 us (5%)
    pallas_call x1, Pallas kernels, shards(): pl.pallas_call(functools.partial(kernel, dims), out_shape=[jax.ShapeDtype...  104 us
    unnamed x7, local copies, waits for them, and re-layouts  4.97 us

profile of v1, /device:TPU:8, one launch (start us, length us, event | category | flops | bytes accessed | tf_op | source)
XLA Modules:
  0.0 109.3 jit_solution(18395927802113611909)
XLA Ops:
  0.6 103.6 %shard_map.85 = (bf16[256,2048]{1,0:T(8,128)(2,1)}, bf16[256,2048]{1,0:T(8,128)(2,1)}, bf16[256,2048]{1,0:T(8,128)(2,1)}) custom-call(bf16[256,2048]{1,0:T(8,128)(2,1)} %q_ref.1, bf16[256,2048]{1,0:T(8,128)(2,1)} %k_ref.1, bf16[256,2048]{1,0:T(8,128)(2,1)} %v_ref.1, bf16[256,2048]{1,0:T(8,128)(2,1)} %cot_ref.1, f32[16,256]{1,0:T(8,128)} %ld_ref.1, ...), custom_call_target="tpu_custom_call" | custom-call | tf_op jit(solution)/shard_map/pallas_call | solution.py:434
  104.3 0.0 copy-start.1
  104.3 2.4 %copy.12 = bf16[256,2048]{1,0:T(8,128)(2,1)} copy(bf16[256,2048]{1,0:T(8,128)(2,1)} %get-tuple-element.6) | data formatting | bytes 2097152
  106.7 0.0 copy-done.1
  106.7 0.0 copy-start
  106.7 1.0 copy.13
  107.7 0.6 copy-done
  108.3 1.0 copy.14
Async XLA Ops:
  104.3 2.4 %copy-start.1 = (bf16[256,2048]{1,0:T(8,128)(2,1)S(1)}, bf16[256,2048]{1,0:T(8,128)(2,1)}, u32[]{:S(2)}) copy-start(bf16[256,2048]{1,0:T(8,128)(2,1)} %get-tuple-element.7) | copy-start | bytes 3145732
  106.7 1.6 %copy-start = (bf16[256,2048]{1,0:T(8,128)(2,1)S(1)}, bf16[256,2048]{1,0:T(8,128)(2,1)}, u32[]{:S(2)}) copy-start(bf16[256,2048]{1,0:T(8,128)(2,1)} %get-tuple-element.8) | copy-start | bytes 3145732

commit v2 on v1

--- a/solution.py
+++ b/solution.py
@@ -28,12 +28,31 @@
     return lax.dot_general(a, b, (((0,), (0,)), ((), ())), preferred_element_type=F32, **kw)
 
 
+LATENCY = {"x": 3.8, "z": 4.2, "y": 3.9}
+CARRY = {"x": 10.5, "z": 5.2, "y": 1.3}
+FORWARD_US, BACKWARD_US = 0.4, 0.6
+
+
+def timetable(chunks):
+    free = {}
+    events = []
+    ready = [0.0] * chunks
+    for level, axis in enumerate(["x", "z", "y", "z", "x"]):
+        link = axis if level else "x"
+        for c in range(chunks):
+            begin = max(free.get(link, 0.0), ready[c])
+            free[link] = begin + CARRY[axis] / chunks
+            ready[c] = free[link] + LATENCY[axis]
+            events.append((ready[c], level, c))
+    return sorted(events)
+
+
 def kernel(
-    dims, q_ref, k_ref, v_ref, cot_ref, ld_ref, gain_ref, gq_ref, gk_ref, gv_ref,
-    cc, crow, kw, vw, qw, mask, sc, of, dob, gkf, gvf, stat,
+    dims, q_in, k_in, v_in, cot_in, ld_in, gain_in, gq_out, gk_out, gv_out,
+    q_ref, k_ref, v_ref, cot_ref, ld_ref, gain_ref, gq_ref, gk_ref, gv_ref, cc, crow, kw, vw, qw, mask, sc, of, dob, gkf, gvf, stat,
     st, xr, tz, zr, uy, yr, ez, er, ex, fin,
     xds, xd, zds, zd, yds, yd, hs, hr,
-    send_sem, recv_sem, dsend, drecv, hsend, hrecv,
+    send_sem, recv_sem, dsend, drecv, hsend, hrecv, in_sem, out_sem,
 ):
     ny, nz, nx, nhd, chunks = dims
     rows = q_ref.shape[0]
@@ -79,6 +98,18 @@
     for device in partners:
         pl.semaphore_signal(barrier, inc=1, device_id=device, device_id_type=MESH)
 
+    def load(i, src, dst):
+        copy = pltpu.make_async_copy(src, dst, in_sem.at[i])
+        copy.start()
+        return copy
+
+    ld_load = load(0, ld_in, ld_ref)
+    k_load = load(1, k_in, k_ref)
+    v_load = load(2, v_in, v_ref)
+    q_load = load(3, q_in, q_ref)
+    cot_load = load(4, cot_in, cot_ref)
+    gain_load = load(5, gain_in, gain_ref)
+
     copies = []
 
     def push(src, dst, send, recv, device):
@@ -97,6 +128,7 @@
     def order(count):
         return sorted(range(1, count), key=lambda i: -min(i, count - i))
 
+    ld_load.wait()
     ld = ld_ref[...]
     r_i = lax.broadcasted_iota(jnp.int32, (rows, rows), 0)
     c_i = lax.broadcasted_iota(jnp.int32, (rows, rows), 1)
@@ -109,11 +141,6 @@
         cc[h] = jnp.broadcast_to(cum_t[:, h:h + 1], (rows, DH))
         xds[h // piece, h % piece] = jnp.broadcast_to(fall_t[:, h:h + 1], (8, DH))
 
-    pl.semaphore_wait(barrier, len(partners))
-
-    xd_copies = [
-        push(xds.at[x_at(i)], xd.at[x], dsend.at[0, i - 1], drecv.at[0, i - 1], x_dev(i)) for i in order(nx)
-    ]
     xd[x] = xds[x]
 
     pending = {}
@@ -136,6 +163,9 @@
     def head_of(c, p, n):
         return p * piece + c * nh + n
 
+    k_load.wait()
+    v_load.wait()
+    decay_copies = {}
     for c in range(chunks):
         for p in range(nx):
             for n in range(nh):
@@ -144,30 +174,41 @@
                 weighted = (k_ref[:, columns(h)].astype(F32) * back).astype(BF16)
                 kw[:, columns(h)] = weighted
                 st[0, c, p, n] = tn(weighted, v_ref[:, columns(h)])
+        if c == 0:
+            pl.semaphore_wait(barrier, len(partners))
+            decay_copies[X_OUT] = [
+                push(xds.at[x_at(i)], xd.at[x], dsend.at[0, i - 1], drecv.at[0, i - 1], x_dev(i)) for i in order(nx)
+            ]
         x_send(0, c)
 
     def z_decays():
-        for copy in xd_copies:
+        for copy in decay_copies[X_OUT]:
             copy.wait_recv()
         total = xd[0]
         for s in range(1, nx):
             total = total * xd[s]
         zds[...] = total
         zd[z] = total
-        return [push(zds, zd.at[z], dsend.at[1, i - 1], drecv.at[1, i - 1], z_dev(i)) for i in order(nz)]
-
-    def y_decays(zd_copies):
-        for copy in zd_copies:
+        decay_copies[Z_OUT] = [
+            push(zds, zd.at[z], dsend.at[1, i - 1], drecv.at[1, i - 1], z_dev(i)) for i in order(nz)
+        ]
+
+    def y_decays():
+        for copy in decay_copies[Z_OUT]:
             copy.wait_recv()
         total = zd[0]
         for s in range(1, nz):
             total = total * zd[s]
         yds[...] = total
         yd[y] = total
-        return [push(yds, yd.at[y], dsend.at[2, i - 1], drecv.at[2, i - 1], y_dev(i)) for i in order(ny)]
+        decay_copies[Y_ALL] = [
+            push(yds, yd.at[y], dsend.at[2, i - 1], drecv.at[2, i - 1], y_dev(i)) for i in order(ny)
+        ]
 
     def x_reduce(way, c):
         arrive(way, X_OUT, c, nx)
+        if way == 0 and c == 0:
+            z_decays()
         for n in range(nh):
             path = list(along(way, nx))
             total = xr[way, c, path[0], n]
@@ -183,6 +224,8 @@
 
     def z_reduce(way, c):
         arrive(way, Z_OUT, c, nz)
+        if way == 0 and c == 0:
+            y_decays()
         for n in range(nh):
             path = list(along(way, nz))
             total = zr[way, c, path[0], n]
@@ -198,6 +241,9 @@
 
     def z_expand(way, c):
         arrive(way, Y_ALL, c, ny)
+        if way == 0 and c == 0:
+            for copy in decay_copies[Y_ALL]:
+                copy.wait_recv()
         for n in range(nh):
             state = jnp.zeros((zr_rows, DH), F32)
             for s in along(way, ny):
@@ -310,40 +356,30 @@
 
         loop(nx * nh, one)
 
-    def scan(way, tasks, last):
-        tasks = iter(tasks)
-        levels = [x_reduce, z_reduce, z_expand, x_expand]
-
-        def fill(count):
-            for task in itertools.islice(tasks, count):
-                task()
-
-        for step in range(chunks + len(levels)):
-            for lag in range(len(levels), -1, -1):
-                c = step - lag
-                if 0 <= c < chunks:
-                    if lag == len(levels):
-                        fill(None)
-                        last(c)
-                    else:
-                        levels[lag](way, c)
-            fill(1)
-        fill(None)
-
-    group = max(heads // chunks, 1)
+    def scan(way, tasks, work, last):
+        levels = [x_reduce, z_reduce, z_expand, x_expand, lambda way, c: last(c)]
+        tasks = list(tasks)
+        now = 0.0
+        for when, level, c in timetable(chunks):
+            while tasks and now + work <= when + 0.5:
+                tasks.pop(0)()
+                now += work
+            if level == len(levels) - 1:
+                while tasks:
+                    tasks.pop(0)()
+            levels[level](way, c)
+            now = max(now, when) + 0.2
+
+    group = max(heads // (2 * chunks), 1)
 
     def forward_group(g):
         loop(group, lambda j: forward_work(g * group + j))
 
     stat[...] = jnp.zeros_like(stat)
-    zd_copies = z_decays()
-    forward_group(0)
-    yd_copies = y_decays(zd_copies)
-    if chunks > 1:
-        forward_group(1)
-    for copy in yd_copies:
-        copy.wait_recv()
-    scan(0, [functools.partial(forward_group, g) for g in range(2, chunks)], enter)
+    q_load.wait()
+    cot_load.wait()
+    gain_load.wait()
+    scan(0, [functools.partial(forward_group, g) for g in range(heads // group)], FORWARD_US * group, enter)
 
     ones = jnp.ones((8, DH), F32)
     pick = lax.broadcasted_iota(jnp.int32, (8, rows), 0) < 4
@@ -375,11 +411,49 @@
         loop(nx * nh, one)
         x_send(1, c)
 
-    backward_work(0)
-    scan(1, [functools.partial(backward_work, c) for c in range(1, chunks)], leave)
+    def flush(i, src, dst):
+        copy = pltpu.make_async_copy(src, dst, out_sem.at[i])
+        copy.start()
+        return copy
+
+    stores = []
+
+    def end(c):
+        if c == 0:
+            stores.append(flush(0, gq_ref, gq_out))
+        leave(c)
+        for p in range(nx):
+            for n in range(nh):
+                h = head_of(c, p, n)
+                stores.append(flush(1 + 2 * h, gk_ref.at[:, columns(h)], gk_out.at[:, columns(h)]))
+                stores.append(flush(2 + 2 * h, gv_ref.at[:, columns(h)], gv_out.at[:, columns(h)]))
+
+    scan(1, [functools.partial(backward_work, c) for c in range(chunks)], BACKWARD_US * nx * nh, end)
+    for copy in stores:
+        copy.wait()
 
     for copy in copies:
         copy.wait_send()
+
+
+SLICES = 4
+
+
+def hand_over(a_in, b_in, c_in, a_out, b_out, c_out, held, in_sem, out_sem):
+    reads, writes = [], []
+    for i, (src, dst) in enumerate([(a_in, a_out), (b_in, b_out), (c_in, c_out)]):
+        rows = src.shape[0] // SLICES
+        for j in range(SLICES):
+            part = pl.ds(j * rows, rows)
+            reads.append(pltpu.make_async_copy(src.at[part], held.at[i, part], in_sem.at[i, j]))
+            writes.append(pltpu.make_async_copy(held.at[i, part], dst.at[part], out_sem.at[i, j]))
+    for read in reads:
+        read.start()
+    for read, write in zip(reads, writes):
+        read.wait()
+        write.start()
+    for write in writes:
+        write.wait()
 
 
 def shards(dims, queries, key_rows, value_rows, cotangent, log_decay, norm_gain):
@@ -394,6 +468,15 @@
     dma = pltpu.SemaphoreType.DMA
     most = max(nx, ny, nz) - 1
     scratch = [
+        vmem((rows, width), BF16),
+        vmem((rows, width), BF16),
+        vmem((rows, width), BF16),
+        vmem((rows, width), BF16),
+        vmem((heads, rows), F32),
+        vmem((1, width), F32),
+        vmem((rows, width), BF16),
+        vmem((rows, width), BF16),
+        vmem((rows, width), BF16),
         vmem((heads, rows, DH), F32),
         vmem((heads, rows), F32),
         vmem((rows, width), BF16),
@@ -430,17 +513,27 @@
         dma((3, most)),
         dma((max(nhd - 1, 1),)),
         dma((max(nhd - 1, 1),)),
+        dma((6,)),
+        dma((1 + 2 * heads,)),
     ]
-    return pl.pallas_call(
+    grads = pl.pallas_call(
         functools.partial(kernel, dims),
         out_shape=[jax.ShapeDtypeStruct((rows, width), BF16)] * 3,
-        in_specs=[pl.BlockSpec(memory_space=pltpu.VMEM)] * 6,
-        out_specs=[pl.BlockSpec(memory_space=pltpu.VMEM)] * 3,
+        in_specs=[pl.BlockSpec(memory_space=pl.ANY)] * 6,
+        out_specs=[pl.BlockSpec(memory_space=pl.ANY)] * 3,
         scratch_shapes=scratch,
         compiler_params=pltpu.CompilerParams(
             collective_id=0, has_side_effects=True, vmem_limit_bytes=56 * 1024 * 1024
         ),
     )(queries, key_rows, value_rows, cotangent, log_decay, norm_gain.reshape(1, width))
+    return pl.pallas_call(
+        hand_over,
+        out_shape=[jax.ShapeDtypeStruct((rows, width), BF16)] * 3,
+        in_specs=[pl.BlockSpec(memory_space=pl.ANY)] * 3,
+        out_specs=[pl.BlockSpec(memory_space=pl.ANY)] * 3,
+        scratch_shapes=[vmem((3, rows, width), BF16), dma((3, SLICES)), dma((3, SLICES))],
+        compiler_params=pltpu.CompilerParams(vmem_limit_bytes=56 * 1024 * 1024),
+    )(*grads)
 
 
 def solution(mesh):

time: 109 us -> 87.4 us (0.80)
  Pallas kernels: 104 us -> 86 us
  local copies, waits for them, and re-layouts: 4.97 us -> 0 us
    pallas_call x1, Pallas kernels: 104 us -> 83.2 us  [shards(): pl.pallas_call(functools.partial(kernel, dims), out_shape=[jax.ShapeDtype...]
    unnamed x7 -> x0, local copies, waits for them, and re-layouts: 4.97 us -> none
    pallas_call x0 -> x1, Pallas kernels: none -> 2.81 us  [shards(): pl.pallas_call(hand_over, out_shape=[jax.ShapeDtypeStruct((rows, width),...]
where the time goes in v2:
time: 87.4 us; the launch traced here: 86.8 us
  Pallas kernels  86 us (98%)
    pallas_call x1, Pallas kernels, shards(): pl.pallas_call(functools.partial(kernel, dims), out_shape=[jax.ShapeDtype...  83.2 us
    pallas_call x1, Pallas kernels, shards(): pl.pallas_call(hand_over, out_shape=[jax.ShapeDtypeStruct((rows, width),...  2.81 us

profile of v2, /device:TPU:8, one launch (start us, length us, event | category | flops | bytes accessed | tf_op | source)
XLA Modules:
  0.0 86.8 jit_solution(6437719481393058112)
XLA Ops:
  0.6 83.2 %shard_map.85 = (bf16[256,2048]{1,0:T(8,128)(2,1)}, bf16[256,2048]{1,0:T(8,128)(2,1)}, bf16[256,2048]{1,0:T(8,128)(2,1)}) custom-call(bf16[256,2048]{1,0:T(8,128)(2,1)} %q_in.1, bf16[256,2048]{1,0:T(8,128)(2,1)} %k_in.1, bf16[256,2048]{1,0:T(8,128)(2,1)} %v_in.1, bf16[256,2048]{1,0:T(8,128)(2,1)} %cot_in.1, f32[16,256]{1,0:T(8,128)} %ld_in.1, f32[1,2048]{1,0:T(1,128)} %bitcast.1), custom_call_target="tpu_custom_call" | custom-call | tf_op jit(solution)/shard_map/pallas_call | solution.py:519
  83.8 2.8 %shard_map.86 = (bf16[256,2048]{1,0:T(8,128)(2,1)}, bf16[256,2048]{1,0:T(8,128)(2,1)}, bf16[256,2048]{1,0:T(8,128)(2,1)}) custom-call(bf16[256,2048]{1,0:T(8,128)(2,1)} %get-tuple-element.6.a_in, bf16[256,2048]{1,0:T(8,128)(2,1)} %get-tuple-element.7.b_in, bf16[256,2048]{1,0:T(8,128)(2,1)} %get-tuple-element.8.c_in), custom_call_target="tpu_custom_call" | custom-call | tf_op jit(solution)/shard_map/pallas_call | solution.py:529

commit v3 on v2

v3 whole, which is shorter than its diff:
```python
import functools

import jax
import jax.numpy as jnp
from jax import lax
from jax.experimental import pallas as pl
from jax.experimental.pallas import tpu as pltpu
from jax.sharding import PartitionSpec as P

eps_norm = 1e-06
MESH = pl.DeviceIdType.MESH
F32, BF16 = jnp.float32, jnp.bfloat16
DH = 128
PARTS = {64: (4, 4, 4), 8: (2, 2, 2)}
X_OUT, Z_OUT, Y_ALL, Z_BACK, X_BACK = range(5)


def nn(a, b, **kw):
    return lax.dot_general(a, b, (((1,), (0,)), ((), ())), preferred_element_type=F32, **kw)


def nt(a, b, **kw):
    return lax.dot_general(a, b, (((1,), (1,)), ((), ())), preferred_element_type=F32, **kw)


def tn(a, b, **kw):
    return lax.dot_general(a, b, (((0,), (0,)), ((), ())), preferred_element_type=F32, **kw)


LATENCY = {"x": 3.5, "z": 4.0, "y": 3.5}
CARRY = {"x": 10.5, "z": 5.2, "y": 1.3}
FORWARD_US, BACKWARD_US, EVENT_US, SLACK_US = 0.22, 0.38, 0.1, 0.3
CUTS = 2


def timetable(chunks):
    free = {}
    events = []
    ready = [0.0] * chunks
    for level, axis in enumerate(["x", "z", "y", "z", "x"]):
        link = axis if level else "x"
        for c in range(chunks):
            begin = max(free.get(link, 0.0), ready[c])
            free[link] = begin + CARRY[axis] / chunks
            ready[c] = free[link] + LATENCY[axis]
            events.append((ready[c], level, c))
    return sorted(events)


def kernel(
    dims, q_in, k_in, v_in, cot_in, ld_in, gain_in, gq_out, gk_out, gv_out,
    q_ref, k_ref, v_ref, cot_ref, ld_ref, gain_ref, gq_ref, gk_ref, gv_ref, cc, crow, kw, vw, qw, mask, sc, of, dob, gkf, gvf, stat,
    st, xr, tz, zr, uy, yr, ez, er, ex, fin,
    xds, xd, zds, zd, yds, yd, hs, hr,
    send_sem, recv_sem, dsend, drecv, hsend, hrecv, in_sem, out_sem,
):
    ny, nz, nx, nhd = dims
    rows = q_ref.shape[0]
    half = rows // 2
    heads = ld_ref.shape[0]
    piece = heads // nx
    chunks = piece * CUTS
    cut = DH // CUTS
    strip = cut // nz
    exact = dict(precision=lax.Precision.HIGHEST)

    me = lax.axis_index("ctx")
    hd = lax.axis_index("head")
    x = lax.rem(me, nx)
    z = lax.rem(lax.div(me, nx), nz)
    y = lax.div(me, nx * nz)

    def x_at(i):
        return lax.rem(x + i, nx)

    def z_at(i):
        return lax.rem(z + i, nz)

    def y_at(i):
        return lax.rem(y + i, ny)

    def x_dev(i):
        return {"ctx": me - x + x_at(i), "head": hd}

    def z_dev(i):
        return {"ctx": me + (z_at(i) - z) * nx, "head": hd}

    def y_dev(i):
        return {"ctx": me + (y_at(i) - y) * (nx * nz), "head": hd}

    def h_dev(i):
        return {"ctx": me, "head": lax.rem(hd + i, nhd)}

    partners = (
        [x_dev(i) for i in range(1, nx)] + [z_dev(i) for i in range(1, nz)]
        + [y_dev(i) for i in range(1, ny)] + [h_dev(i) for i in range(1, nhd)]
    )
    barrier = pltpu.get_barrier_semaphore()
    for device in partners:
        pl.semaphore_signal(barrier, inc=1, device_id=device, device_id_type=MESH)

    def load(i, src, dst):
        copy = pltpu.make_async_copy(src, dst, in_sem.at[i])
        copy.start()
        return copy

    ld_load = load(0, ld_in, ld_ref)
    k_load = load(1, k_in, k_ref)
    v_load = load(2, v_in, v_ref)
    q_load = load(3, q_in, q_ref)
    cot_load = load(4, cot_in, cot_ref)
    gain_load = load(5, gain_in, gain_ref)

    def push(src, dst, send, recv, device):
        copy = pltpu.make_async_remote_copy(
            src_ref=src, dst_ref=dst, send_sem=send, recv_sem=recv, device_id=device, device_id_type=MESH
        )
        copy.start()
        return copy

    def columns(h):
        if isinstance(h, int):
            return pl.ds(h * DH, DH)
        return pl.ds(pl.multiple_of(h * DH, DH), DH)

    def order(count):
        return sorted(range(1, count), key=lambda i: -min(i, count - i))

    ld_load.wait()
    ld = ld_ref[...]
    r_i = lax.broadcasted_iota(jnp.int32, (rows, rows), 0)
    c_i = lax.broadcasted_iota(jnp.int32, (rows, rows), 1)
    crow[...] = nn(ld, (r_i <= c_i).astype(F32), **exact)
    cum_t = nt((r_i >= c_i).astype(F32), ld, **exact)
    end_t = cum_t[rows - 1:rows, :]
    bg_t = jnp.exp(end_t - cum_t)
    fall_t = jnp.exp(end_t)
    for h in range(heads):
        cc[h] = jnp.broadcast_to(cum_t[:, h:h + 1], (rows, DH))
        xds[h // piece, h % piece] = jnp.broadcast_to(fall_t[:, h:h + 1], (8, DH))

    xd[x] = xds[x]

    def x_send(way, c):
        for i in order(nx):
            push(
                st.at[way, c, x_at(i)], xr.at[way, c, x],
                send_sem.at[way, X_OUT, c], recv_sem.at[way, X_OUT, c], x_dev(i),
            )
        xr[way, c, x] = st[way, c, x]

    def arrive(way, level, c):
        size = sizes(level, way, c)
        pltpu.make_async_copy(size, size, recv_sem.at[way, level, c]).wait()

    def leave_behind(way):
        for level in range(5):
            for c in range(chunks):
                size = sizes(level, way, c)
                pltpu.make_async_copy(size, size, send_sem.at[way, level, c]).wait()

    def sizes(level, way, c):
        if level in (X_OUT, X_BACK):
            return xr.at[way, c, pl.ds(0, nx - 1)]
        return (zr if level in (Z_OUT, Z_BACK) else yr).at[way, c, pl.ds(0, (ny if level == Y_ALL else nz) - 1)]

    def along(way, count):
        return range(count) if way == 0 else range(count - 1, -1, -1)

    def keep(way, g, p, state):
        for u in range(CUTS):
            st[way, g * CUTS + u, p] = state[u * cut:(u + 1) * cut]

    k_load.wait()
    v_load.wait()
    decay_copies = {}
    for g in range(piece):
        for p in range(nx):
            h = p * piece + g
            back = jnp.broadcast_to(bg_t[:, h:h + 1], (rows, DH))
            weighted = (k_ref[:, columns(h)].astype(F32) * back).astype(BF16)
            kw[:, columns(h)] = weighted
            keep(0, g, p, tn(weighted, v_ref[:, columns(h)]))
        if g == 0:
            pl.semaphore_wait(barrier, len(partners))
            decay_copies[X_OUT] = [
                push(xds.at[x_at(i)], xd.at[x], dsend.at[0, i - 1], drecv.at[0, i - 1], x_dev(i)) for i in order(nx)
            ]
        for u in range(CUTS):
            x_send(0, g * CUTS + u)

    def z_decays():
        for copy in decay_copies[X_OUT]:
            copy.wait_recv()
        total = xd[0]
        for s in range(1, nx):
            total = total * xd[s]
        zds[...] = total
        zd[z] = total
        decay_copies[Z_OUT] = [
            push(zds, zd.at[z], dsend.at[1, i - 1], drecv.at[1, i - 1], z_dev(i)) for i in order(nz)
        ]

    def y_decays():
        for copy in decay_copies[Z_OUT]:
            copy.wait_recv()
        total = zd[0]
        for s in range(1, nz):
            total = total * zd[s]
        yds[...] = total
        yd[y] = total
        decay_copies[Y_ALL] = [
            push(yds, yd.at[y], dsend.at[2, i - 1], drecv.at[2, i - 1], y_dev(i)) for i in order(ny)
        ]

    def x_reduce(way, c):
        g = c // CUTS
        if way == 0 and c == 0:
            z_decays()
        arrive(way, X_OUT, c)
        path = list(along(way, nx))
        total = xr[way, c, path[0]]
        for s in path[1:]:
            total = xd[s, g, 0:1, :] * total + xr[way, c, s]
        tz[way, c] = total
        for i in order(nz):
            push(
                tz.at[way, c, pl.ds(z_at(i) * strip, strip)], zr.at[way, c, z],
                send_sem.at[way, Z_OUT, c], recv_sem.at[way, Z_OUT, c], z_dev(i),
            )
        zr[way, c, z] = tz[way, c, pl.ds(z * strip, strip)]

    def z_reduce(way, c):
        g = c // CUTS
        if way == 0 and c == 0:
            y_decays()
        arrive(way, Z_OUT, c)
        path = list(along(way, nz))
        total = zr[way, c, path[0]]
        for s in path[1:]:
            total = zd[s, g, 0:1, :] * total + zr[way, c, s]
        uy[way, c] = total
        for i in order(ny):
            push(
                uy.at[way, c], yr.at[way, c, y],
                send_sem.at[way, Y_ALL, c], recv_sem.at[way, Y_ALL, c], y_dev(i),
            )
        yr[way, c, y] = total

    def z_expand(way, c):
        g = c // CUTS
        if way == 0 and c == 0:
            for copy in decay_copies[Y_ALL]:
                copy.wait_recv()
        arrive(way, Y_ALL, c)
        state = jnp.zeros((strip, DH), F32)
        for s in along(way, ny):
            longer = yd[s, g, 0:1, :] * state + yr[way, c, s]
            before = (s < y) if way == 0 else (s > y)
            state = jnp.where(before, longer, state)
        for s in along(way, nz):
            ez[way, c, s] = state
            state = zd[s, g, 0:1, :] * state + zr[way, c, s]
        for i in order(nz):
            push(
                ez.at[way, c, z_at(i)], er.at[way, c, pl.ds(z * strip, strip)],
                send_sem.at[way, Z_BACK, c], recv_sem.at[way, Z_BACK, c], z_dev(i),
            )
        er[way, c, pl.ds(z * strip, strip)] = ez[way, c, z]

    def x_expand(way, c):
        g, u = c // CUTS, c % CUTS
        arrive(way, Z_BACK, c)
        state = er[way, c]
        for s in along(way, nx):
            ex[way, c, s] = state
            state = xd[s, g, 0:1, :] * state + xr[way, c, s]
        here = pl.ds(u * cut, cut)
        for i in order(nx):
            push(
                ex.at[way, c, x_at(i)], fin.at[way, g, x, here],
                send_sem.at[way, X_BACK, c], recv_sem.at[way, X_BACK, c], x_dev(i),
            )
        fin[way, g, x, here] = ex[way, c, x]

    def arrived(way, g):
        for u in range(CUTS):
            arrive(way, X_BACK, g * CUTS + u)

    def loop(count, body):
        pair = 2 if count % 2 == 0 else 1

        def step(j, carry):
            for u in range(pair):
                body(j * pair + u)
            return carry

        lax.fori_loop(0, count // pair, step, 0)

    lower = (
        lax.broadcasted_iota(jnp.int32, (half, half), 0) >= lax.broadcasted_iota(jnp.int32, (half, half), 1)
    )

    def forward_work(h):
        here = columns(h)
        col = cc[h]
        line = crow[pl.ds(h, 1), :]
        m00 = jnp.where(lower, jnp.exp(jnp.minimum(col[:half] - line[:, :half], 0.0)), 0.0)
        m10 = jnp.exp(jnp.minimum(col[half:] - line[:, :half], 0.0))
        m11 = jnp.where(lower, jnp.exp(jnp.minimum(col[half:] - line[:, half:], 0.0)), 0.0)
        mask[h, 0], mask[h, 1], mask[h, 2] = m00, m10, m11
        q, k, v = q_ref[:, here], k_ref[:, here], v_ref[:, here]
        top = (nt(q[:half], k[:half]) * m00).astype(BF16)
        bottom = nt(q[half:], k)
        low_left = (bottom[:, :half] * m10).astype(BF16)
        low_right = (bottom[:, half:] * m11).astype(BF16)
        sc[h, 0], sc[h, 1], sc[h, 2] = top, low_left, low_right
        of[:half, here] = nn(top, v[:half])
        of[half:, here] = nn(low_left, v[:half]) + nn(low_right, v[half:])
        qw[:, here] = (q.astype(F32) * jnp.exp(col)).astype(BF16)
        vw[:, here] = (v.astype(F32) * jnp.exp(col[rows - 1:rows, :] - col)).astype(BF16)

    def enter(g):
        arrived(0, g)

        def one(p):
            here = columns(p * piece + g)
            out = of[:, here] + nn(qw[:, here], fin[0, g, p].astype(BF16))
            of[:, here] = out
            scaled = gain_ref[:, here] * cot_ref[:, here].astype(F32)
            stat[0] += out * out
            stat[1] += out * scaled

        loop(nx, one)

    def backward_work(g):
        def one(p):
            h = p * piece + g
            here = columns(h)
            d_out = dob[:, here]
            q, k, v = q_ref[:, here], k_ref[:, here], v_ref[:, here]
            top = (nt(d_out[:half], v[:half]) * mask[h, 0]).astype(BF16)
            bottom = nt(d_out[half:], v)
            low_left = (bottom[:, :half] * mask[h, 1]).astype(BF16)
            low_right = (bottom[:, half:] * mask[h, 2]).astype(BF16)
            entry = fin[0, g, p].astype(BF16)
            weighted = (d_out.astype(F32) * jnp.exp(cc[h])).astype(BF16)
            cross = nt(weighted, entry)
            gq_ref[:half, here] = (nn(top, k[:half]) + cross[:half]).astype(BF16)
            gq_ref[half:, here] = (nn(low_left, k[:half]) + nn(low_right, k[half:]) + cross[half:]).astype(BF16)
            gkf[:half, here] = tn(top, q[:half]) + tn(low_left, q[half:])
            gkf[half:, here] = tn(low_right, q[half:])
            gvf[:half, here] = tn(sc[h, 0], d_out[:half]) + tn(sc[h, 1], d_out[half:])
            gvf[half:, here] = tn(sc[h, 2], d_out[half:])

        loop(nx, one)

    def leave(g):
        arrived(1, g)

        def one(p):
            here = columns(p * piece + g)
            low = fin[1, g, p].astype(BF16)
            gk_ref[:, here] = (gkf[:, here] + nt(vw[:, here], low)).astype(BF16)
            gv_ref[:, here] = (gvf[:, here] + nn(kw[:, here], low)).astype(BF16)

        loop(nx, one)

    def scan(way, tasks, work, last):
        levels = [x_reduce, z_reduce, z_expand, x_expand]
        tasks = list(tasks)
        now = 0.0
        for when, level, c in timetable(chunks):
            while tasks and now + work <= when + SLACK_US:
                tasks.pop(0)()
                now += work
            if level < len(levels):
                levels[level](way, c)
                now = max(now, when) + EVENT_US
            elif c % CUTS == CUTS - 1:
                while tasks:
                    tasks.pop(0)()
                last(c // CUTS)

    def forward_group(g):
        loop(nx, lambda p: forward_work(p * piece + g))

    stat[...] = jnp.zeros_like(stat)
    q_load.wait()
    cot_load.wait()
    gain_load.wait()
    scan(0, [functools.partial(forward_group, g) for g in range(piece)], FORWARD_US * nx, enter)

    ones = jnp.ones((8, DH), F32)
    pick = lax.broadcasted_iota(jnp.int32, (8, rows), 0) < 4
    hs[...] = jnp.where(pick, nt(ones, stat[0], **exact), nt(ones, stat[1], **exact))
    hr[hd] = hs[...]
    h_copies = [push(hs, hr.at[hd], hsend.at[i - 1], hrecv.at[i - 1], h_dev(i)) for i in order(nhd)]
    for copy in h_copies:
        copy.wait_recv()
    both = hr[0]
    for s in range(1, nhd):
        both = both + hr[s]
    features = nhd * q_ref.shape[1]
    square_sum, inner_sum = both[0:1, :], both[4:5, :]
    root_mean = jnp.sqrt(square_sum / features + eps_norm)
    scales = jnp.where(pick, 1.0 / root_mean, inner_sum / (features * root_mean * root_mean * root_mean))
    where = lax.broadcasted_iota(jnp.int32, (8, DH), 0)
    stat[0] = tn(scales, (where == 0).astype(F32), **exact)
    stat[1] = tn(scales, (where == 4).astype(F32), **exact)

    for g in range(piece):
        def one(p, g=g):
            here = columns(p * piece + g)
            scaled = gain_ref[:, here] * cot_ref[:, here].astype(F32)
            d_out = (scaled * stat[0] - of[:, here] * stat[1]).astype(BF16)
            dob[:, here] = d_out
            keep(1, g, p, tn(qw[:, here], d_out))

        loop(nx, one)
        for u in range(CUTS):
            x_send(1, g * CUTS + u)

    def flush(i, src, dst):
        copy = pltpu.make_async_copy(src, dst, out_sem.at[i])
        copy.start()
        return copy

    stores = []

    def end(g):
        if g == 0:
            stores.append(flush(0, gq_ref, gq_out))
            leave_behind(0)
            for level in decay_copies.values():
                for copy in level:
                    copy.wait_send()
            for copy in h_copies:
                copy.wait_send()
        leave(g)
        for p in range(nx):
            h = p * piece + g
            stores.append(flush(1 + 2 * h, gk_ref.at[:, columns(h)], gk_out.at[:, columns(h)]))
            stores.append(flush(2 + 2 * h, gv_ref.at[:, columns(h)], gv_out.at[:, columns(h)]))

    scan(1, [functools.partial(backward_work, g) for g in range(piece)], BACKWARD_US * nx, end)
    leave_behind(1)
    for copy in stores:
        copy.wait()


SLICES = 4


def hand_over(a_in, b_in, c_in, a_out, b_out, c_out, sem):
    copies = []
    for i, (src, dst) in enumerate([(a_in, a_out), (b_in, b_out), (c_in, c_out)]):
        rows = src.shape[0] // SLICES
        for j in range(SLICES):
            part = pl.ds(j * rows, rows)
            copies.append(pltpu.make_async_copy(src.at[part], dst.at[part], sem.at[i, j]))
    for copy in copies:
        copy.start()
    for copy in copies:
        copy.wait()


def shards(dims, queries, key_rows, value_rows, cotangent, log_decay, norm_gain):
    ny, nz, nx, nhd = dims
    rows, width = queries.shape
    heads = log_decay.shape[0]
    piece = heads // nx
    chunks = piece * CUTS
    cut = DH // CUTS
    strip = cut // nz
    half = rows // 2
    vmem = pltpu.VMEM
    dma = pltpu.SemaphoreType.DMA
    most = max(nx, ny, nz) - 1
    scratch = [
        vmem((rows, width), BF16),
        vmem((rows, width), BF16),
        vmem((rows, width), BF16),
        vmem((rows, width), BF16),
        vmem((heads, rows), F32),
        vmem((1, width), F32),
        vmem((rows, width), BF16),
        vmem((rows, width), BF16),
        vmem((rows, width), BF16),
        vmem((heads, rows, DH), F32),
        vmem((heads, rows), F32),
        vmem((rows, width), BF16),
        vmem((rows, width), BF16),
        vmem((rows, width), BF16),
        vmem((heads, 3, half, half), F32),
        vmem((heads, 3, half, half), BF16),
        vmem((rows, width), F32),
        vmem((rows, width), BF16),
        vmem((rows, width), F32),
        vmem((rows, width), F32),
        vmem((2, rows, DH), F32),
        vmem((2, chunks, nx, cut, DH), F32),
        vmem((2, chunks, nx, cut, DH), F32),
        vmem((2, chunks, cut, DH), F32),
        vmem((2, chunks, nz, strip, DH), F32),
        vmem((2, chunks, strip, DH), F32),
        vmem((2, chunks, ny, strip, DH), F32),
        vmem((2, chunks, nz, strip, DH), F32),
        vmem((2, chunks, cut, DH), F32),
        vmem((2, chunks, nx, cut, DH), F32),
        vmem((2, piece, nx, DH, DH), F32),
        vmem((nx, piece, 8, DH), F32),
        vmem((nx, piece, 8, DH), F32),
        vmem((piece, 8, DH), F32),
        vmem((nz, piece, 8, DH), F32),
        vmem((piece, 8, DH), F32),
        vmem((ny, piece, 8, DH), F32),
        vmem((8, rows), F32),
        vmem((nhd, 8, rows), F32),
        dma((2, 5, chunks)),
        dma((2, 5, chunks)),
        dma((3, most)),
        dma((3, most)),
        dma((max(nhd - 1, 1),)),
        dma((max(nhd - 1, 1),)),
        dma((6,)),
        dma((1 + 2 * heads,)),
    ]
    grads = pl.pallas_call(
        functools.partial(kernel, dims),
        out_shape=[jax.ShapeDtypeStruct((rows, width), BF16)] * 3,
        in_specs=[pl.BlockSpec(memory_space=pltpu.HBM)] * 6,
        out_specs=[pl.BlockSpec(memory_space=pl.ANY)] * 3,
        scratch_shapes=scratch,
        compiler_params=pltpu.CompilerParams(
            collective_id=0, has_side_effects=True, vmem_limit_bytes=50 * 1024 * 1024
        ),
    )(queries, key_rows, value_rows, cotangent, log_decay, norm_gain.reshape(1, width))
    return pl.pallas_call(
        hand_over,
        out_shape=[jax.ShapeDtypeStruct((rows, width), BF16)] * 3,
        in_specs=[pl.BlockSpec(memory_space=pl.ANY)] * 3,
        out_specs=[pl.BlockSpec(memory_space=pl.ANY)] * 3,
        scratch_shapes=[dma((3, SLICES))],
        compiler_params=pltpu.CompilerParams(vmem_limit_bytes=8 * 1024 * 1024),
    )(*grads)


def solution(mesh):
    ny, nz, nx = PARTS[mesh.shape["ctx"]]
    dims = (ny, nz, nx, mesh.shape["head"])
    in_specs = (
        P("ctx", "head"),
        P("ctx", "head"),
        P("ctx", "head"),
        P("ctx", "head"),
        P("head", "ctx"),
        P("head"),
    )
    out_specs = (P("ctx", "head"), P("ctx", "head"), P("ctx", "head"))
    return jax.shard_map(
        functools.partial(shards, dims), mesh=mesh, in_specs=in_specs, out_specs=out_specs, check_vma=False
    )
```

time: 87.4 us -> 81.2 us (0.929)
  Pallas kernels: 86 us -> 78.9 us
  local copies, waits for them, and re-layouts: 0 us -> 1.41 us
    pallas_call x1, Pallas kernels: 83.2 us -> 77.1 us  [shards(): pl.pallas_call(functools.partial(kernel, dims), out_shape=[jax.ShapeDtype...]
    unnamed x0 -> x4, local copies, waits for them, and re-layouts: none -> 1.41 us
    pallas_call x1, Pallas kernels: 2.81 us -> 1.76 us  [shards(): pl.pallas_call(hand_over, out_shape=[jax.ShapeDtypeStruct((rows, width),...]
where the time goes in v3:
time: 81.2 us; the launch traced here: 80.9 us
  Pallas kernels  78.9 us (97%)
  local copies, waits for them, and re-layouts  1.41 us (2%)
    pallas_call x1, Pallas kernels, shards(): pl.pallas_call(functools.partial(kernel, dims), out_shape=[jax.ShapeDtype...  77.1 us
    pallas_call x1, Pallas kernels, shards(): pl.pallas_call(hand_over, out_shape=[jax.ShapeDtypeStruct((rows, width),...  1.76 us

profile of v3, /device:TPU:8, one launch (start us, length us, event | category | flops | bytes accessed | tf_op | source)
XLA Modules:
  0.0 80.9 jit_solution(12091410769561766219)
XLA Ops:
  0.6 0.0 copy-start
  0.6 0.7 copy-done
  1.4 0.0 copy-start.1
  1.4 0.7 copy-done.1
  2.0 77.1 %shard_map.85 = (bf16[256,2048]{1,0:T(8,128)(2,1)S(1)}, bf16[256,2048]{1,0:T(8,128)(2,1)S(1)}, bf16[256,2048]{1,0:T(8,128)(2,1)S(1)}) custom-call(bf16[256,2048]{1,0:T(8,128)(2,1)} %q_in.1, bf16[256,2048]{1,0:T(8,128)(2,1)} %k_in.1, bf16[256,2048]{1,0:T(8,128)(2,1)} %v_in.1, bf16[256,2048]{1,0:T(8,128)(2,1)} %cot_in.1, f32[16,256]{1,0:T(8,128)S(1)} %copy-done, ...), custom_call_target="tpu_custom_call" | custom-call | tf_op jit(solution)/shard_map/pallas_call | solution.py:529
  79.2 1.8 %shard_map.86 = (bf16[256,2048]{1,0:T(8,128)(2,1)}, bf16[256,2048]{1,0:T(8,128)(2,1)}, bf16[256,2048]{1,0:T(8,128)(2,1)}) custom-call(bf16[256,2048]{1,0:T(8,128)(2,1)S(1)} %get-tuple-element.6.a_in, bf16[256,2048]{1,0:T(8,128)(2,1)S(1)} %get-tuple-element.7.b_in, bf16[256,2048]{1,0:T(8,128)(2,1)S(1)} %get-tuple-element.8.c_in), custom_call_target="tpu_custom_call" | custom-call | tf_op jit(solution)/shard_map/pallas_call | solution.py:539
Async XLA Ops:
  0.6 0.7 copy-start
  1.4 0.7 copy-start.1

commit v4 on v3

--- a/solution.py
+++ b/solution.py
@@ -29,7 +29,7 @@
 
 LATENCY = {"x": 3.5, "z": 4.0, "y": 3.5}
 CARRY = {"x": 10.5, "z": 5.2, "y": 1.3}
-FORWARD_US, BACKWARD_US, EVENT_US, SLACK_US = 0.22, 0.38, 0.1, 0.3
+FORWARD_US, BACKWARD_US, EVENT_US, SLACK_US = 0.22, 0.38, 0.2, 0.3
 CUTS = 2
 
 
@@ -48,11 +48,11 @@
 
 
 def kernel(
-    dims, q_in, k_in, v_in, cot_in, ld_in, gain_in, gq_out, gk_out, gv_out,
-    q_ref, k_ref, v_ref, cot_ref, ld_ref, gain_ref, gq_ref, gk_ref, gv_ref, cc, crow, kw, vw, qw, mask, sc, of, dob, gkf, gvf, stat,
+    dims, q_in, k_in, v_in, cot_in, ld_in, gain_in, gq_ref, gk_ref, gv_ref,
+    q_ref, k_ref, v_ref, cot_ref, ld_ref, gain_ref, cc, crow, kw, vw, qw, mask, sc, of, dob, gkf, gvf, stat,
     st, xr, tz, zr, uy, yr, ez, er, ex, fin,
     xds, xd, zds, zd, yds, yd, hs, hr,
-    send_sem, recv_sem, dsend, drecv, hsend, hrecv, in_sem, out_sem,
+    send_sem, recv_sem, dsend, drecv, hsend, hrecv, in_sem,
 ):
     ny, nz, nx, nhd = dims
     rows = q_ref.shape[0]
@@ -333,27 +333,23 @@
 
         loop(nx, one)
 
-    def backward_work(g):
-        def one(p):
-            h = p * piece + g
-            here = columns(h)
-            d_out = dob[:, here]
-            q, k, v = q_ref[:, here], k_ref[:, here], v_ref[:, here]
-            top = (nt(d_out[:half], v[:half]) * mask[h, 0]).astype(BF16)
-            bottom = nt(d_out[half:], v)
-            low_left = (bottom[:, :half] * mask[h, 1]).astype(BF16)
-            low_right = (bottom[:, half:] * mask[h, 2]).astype(BF16)
-            entry = fin[0, g, p].astype(BF16)
-            weighted = (d_out.astype(F32) * jnp.exp(cc[h])).astype(BF16)
-            cross = nt(weighted, entry)
-            gq_ref[:half, here] = (nn(top, k[:half]) + cross[:half]).astype(BF16)
-            gq_ref[half:, here] = (nn(low_left, k[:half]) + nn(low_right, k[half:]) + cross[half:]).astype(BF16)
-            gkf[:half, here] = tn(top, q[:half]) + tn(low_left, q[half:])
-            gkf[half:, here] = tn(low_right, q[half:])
-            gvf[:half, here] = tn(sc[h, 0], d_out[:half]) + tn(sc[h, 1], d_out[half:])
-            gvf[half:, here] = tn(sc[h, 2], d_out[half:])
-
-        loop(nx, one)
+    def backward_work(h):
+        here = columns(h)
+        d_out = dob[:, here]
+        q, k, v = q_ref[:, here], k_ref[:, here], v_ref[:, here]
+        top = (nt(d_out[:half], v[:half]) * mask[h, 0]).astype(BF16)
+        bottom = nt(d_out[half:], v)
+        low_left = (bottom[:, :half] * mask[h, 1]).astype(BF16)
+        low_right = (bottom[:, half:] * mask[h, 2]).astype(BF16)
+        entry = fin[0, lax.rem(h, piece), lax.div(h, piece)].astype(BF16)
+        weighted = (d_out.astype(F32) * jnp.exp(cc[h])).astype(BF16)
+        cross = nt(weighted, entry)
+        gq_ref[:half, here] = (nn(top, k[:half]) + cross[:half]).astype(BF16)
+        gq_ref[half:, here] = (nn(low_left, k[:half]) + nn(low_right, k[half:]) + cross[half:]).astype(BF16)
+        gkf[:half, here] = tn(top, q[:half]) + tn(low_left, q[half:])
+        gkf[half:, here] = tn(low_right, q[half:])
+        gvf[:half, here] = tn(sc[h, 0], d_out[:half]) + tn(sc[h, 1], d_out[half:])
+        gvf[half:, here] = tn(sc[h, 2], d_out[half:])
 
     def leave(g):
         arrived(1, g)
@@ -371,25 +367,25 @@
         tasks = list(tasks)
         now = 0.0
         for when, level, c in timetable(chunks):
-            while tasks and now + work <= when + SLACK_US:
-                tasks.pop(0)()
-                now += work
             if level < len(levels):
+                while tasks and now + work <= when + SLACK_US:
+                    tasks.pop(0)()
+                    now += work
                 levels[level](way, c)
                 now = max(now, when) + EVENT_US
-            elif c % CUTS == CUTS - 1:
-                while tasks:
-                    tasks.pop(0)()
-                last(c // CUTS)
-
-    def forward_group(g):
-        loop(nx, lambda p: forward_work(p * piece + g))
+        for task in tasks:
+            task()
+        for g in range(piece):
+            last(g)
+
+    def some(work):
+        return [functools.partial(loop, 2, lambda u, j=j: work(2 * j + u)) for j in range(heads // 2)]
 
     stat[...] = jnp.zeros_like(stat)
     q_load.wait()
     cot_load.wait()
     gain_load.wait()
-    scan(0, [functools.partial(forward_group, g) for g in range(piece)], FORWARD_US * nx, enter)
+    scan(0, some(forward_work), FORWARD_US * 2, enter)
 
     ones = jnp.ones((8, DH), F32)
     pick = lax.broadcasted_iota(jnp.int32, (8, rows), 0) < 4
@@ -421,16 +417,8 @@
         for u in range(CUTS):
             x_send(1, g * CUTS + u)
 
-    def flush(i, src, dst):
-        copy = pltpu.make_async_copy(src, dst, out_sem.at[i])
-        copy.start()
-        return copy
-
-    stores = []
-
     def end(g):
         if g == 0:
-            stores.append(flush(0, gq_ref, gq_out))
             leave_behind(0)
             for level in decay_copies.values():
                 for copy in level:
@@ -438,15 +426,9 @@
             for copy in h_copies:
                 copy.wait_send()
         leave(g)
-        for p in range(nx):
-            h = p * piece + g
-            stores.append(flush(1 + 2 * h, gk_ref.at[:, columns(h)], gk_out.at[:, columns(h)]))
-            stores.append(flush(2 + 2 * h, gv_ref.at[:, columns(h)], gv_out.at[:, columns(h)]))
-
-    scan(1, [functools.partial(backward_work, g) for g in range(piece)], BACKWARD_US * nx, end)
+
+    scan(1, some(backward_work), BACKWARD_US * 2, end)
     leave_behind(1)
-    for copy in stores:
-        copy.wait()
 
 
 SLICES = 4
@@ -484,9 +466,6 @@
         vmem((rows, width), BF16),
         vmem((heads, rows), F32),
         vmem((1, width), F32),
-        vmem((rows, width), BF16),
-        vmem((rows, width), BF16),
-        vmem((rows, width), BF16),
         vmem((heads, rows, DH), F32),
         vmem((heads, rows), F32),
         vmem((rows, width), BF16),
@@ -524,18 +503,20 @@
         dma((max(nhd - 1, 1),)),
         dma((max(nhd - 1, 1),)),
         dma((6,)),
-        dma((1 + 2 * heads,)),
     ]
     grads = pl.pallas_call(
         functools.partial(kernel, dims),
-        out_shape=[jax.ShapeDtypeStruct((rows, width), BF16)] * 3,
+        out_shape=[pltpu.VMEM((rows, width), BF16)] * 3,
         in_specs=[pl.BlockSpec(memory_space=pltpu.HBM)] * 6,
-        out_specs=[pl.BlockSpec(memory_space=pl.ANY)] * 3,
+        out_specs=[pl.BlockSpec(memory_space=pltpu.VMEM)] * 3,
         scratch_shapes=scratch,
         compiler_params=pltpu.CompilerParams(
             collective_id=0, has_side_effects=True, vmem_limit_bytes=50 * 1024 * 1024
         ),
-    )(queries, key_rows, value_rows, cotangent, log_decay, norm_gain.reshape(1, width))
+    )(*(
+        pltpu.with_memory_space_constraint(array, pltpu.HBM)
+        for array in (queries, key_rows, value_rows, cotangent, log_decay, norm_gain.reshape(1, width))
+    ))
     return pl.pallas_call(
         hand_over,
         out_shape=[jax.ShapeDtypeStruct((rows, width), BF16)] * 3,

time: 81.2 us -> 79.7 us (0.982)
  local copies, waits for them, and re-layouts: 1.41 us -> 0 us
    unnamed x4 -> x0, local copies, waits for them, and re-layouts: 1.41 us -> none
where the time goes in v4:
time: 79.7 us; the launch traced here: 79.5 us
  Pallas kernels  78.7 us (99%)
  between operations  0.8 us (1%)
    pallas_call x1, Pallas kernels, shards(): pl.pallas_call(functools.partial(kernel, dims), out_shape=[pltpu.VMEM((ro...  76.9 us
    pallas_call x1, Pallas kernels, shards(): pl.pallas_call(hand_over, out_shape=[jax.ShapeDtypeStruct((rows, width),...  1.76 us

profile of v4, /device:TPU:8, one launch (start us, length us, event | category | flops | bytes accessed | tf_op | source)
XLA Modules:
  0.0 79.5 jit_solution(17040523496624297405)
XLA Ops:
  0.6 76.9 %shard_map.85 = (bf16[256,2048]{1,0:T(8,128)(2,1)S(1)}, bf16[256,2048]{1,0:T(8,128)(2,1)S(1)}, bf16[256,2048]{1,0:T(8,128)(2,1)S(1)}) custom-call(bf16[256,2048]{1,0:T(8,128)(2,1)} %q_in.1, bf16[256,2048]{1,0:T(8,128)(2,1)} %k_in.1, bf16[256,2048]{1,0:T(8,128)(2,1)} %v_in.1, bf16[256,2048]{1,0:T(8,128)(2,1)} %cot_in.1, f32[16,256]{1,0:T(8,128)} %ld_in.1, ...), custom_call_target="tpu_custom_call" | custom-call | tf_op jit(solution)/shard_map/pallas_call | solution.py:507
  77.6 1.8 %shard_map.86 = (bf16[256,2048]{1,0:T(8,128)(2,1)}, bf16[256,2048]{1,0:T(8,128)(2,1)}, bf16[256,2048]{1,0:T(8,128)(2,1)}) custom-call(bf16[256,2048]{1,0:T(8,128)(2,1)S(1)} %get-tuple-element.6.a_in, bf16[256,2048]{1,0:T(8,128)(2,1)S(1)} %get-tuple-element.7.b_in, bf16[256,2048]{1,0:T(8,128)(2,1)S(1)} %get-tuple-element.8.c_in), custom_call_target="tpu_custom_call" | custom-call | tf_op jit(solution)/shard_map/pallas_call | solution.py:520

commit v5 on v4

--- a/solution.py
+++ b/solution.py
@@ -288,7 +288,7 @@
             arrive(way, X_BACK, g * CUTS + u)
 
     def loop(count, body):
-        pair = 2 if count % 2 == 0 else 1
+        pair = next(size for size in (4, 2, 1) if count % size == 0)
 
         def step(j, carry):
             for u in range(pair):
@@ -323,15 +323,14 @@
     def enter(g):
         arrived(0, g)
 
-        def one(p):
+        squares, inners = stat[0], stat[1]
+        for p in range(nx):
             here = columns(p * piece + g)
             out = of[:, here] + nn(qw[:, here], fin[0, g, p].astype(BF16))
             of[:, here] = out
-            scaled = gain_ref[:, here] * cot_ref[:, here].astype(F32)
-            stat[0] += out * out
-            stat[1] += out * scaled
-
-        loop(nx, one)
+            squares += out * out
+            inners += out * (gain_ref[:, here] * cot_ref[:, here].astype(F32))
+        stat[0], stat[1] = squares, inners
 
     def backward_work(h):
         here = columns(h)

time: 79.7 us -> 79 us (level)
  no operation moved by 1% of the time
where the time goes in v5:
time: 79 us; the launch traced here: 78.8 us
  Pallas kernels  78 us (99%)
  between operations  0.8 us (1%)
    pallas_call x1, Pallas kernels, shards(): pl.pallas_call(functools.partial(kernel, dims), out_shape=[pltpu.VMEM((ro...  76.3 us
    pallas_call x1, Pallas kernels, shards(): pl.pallas_call(hand_over, out_shape=[jax.ShapeDtypeStruct((rows, width),...  1.76 us

profile of v5, /device:TPU:8, one launch (start us, length us, event | category | flops | bytes accessed | tf_op | source)
XLA Modules:
  0.0 78.8 jit_solution(6962942809197516868)
XLA Ops:
  0.6 76.3 %shard_map.85 = (bf16[256,2048]{1,0:T(8,128)(2,1)S(1)}, bf16[256,2048]{1,0:T(8,128)(2,1)S(1)}, bf16[256,2048]{1,0:T(8,128)(2,1)S(1)}) custom-call(bf16[256,2048]{1,0:T(8,128)(2,1)} %q_in.1, bf16[256,2048]{1,0:T(8,128)(2,1)} %k_in.1, bf16[256,2048]{1,0:T(8,128)(2,1)} %v_in.1, bf16[256,2048]{1,0:T(8,128)(2,1)} %cot_in.1, f32[16,256]{1,0:T(8,128)} %ld_in.1, ...), custom_call_target="tpu_custom_call" | custom-call | tf_op jit(solution)/shard_map/pallas_call | solution.py:506
  76.9 1.8 %shard_map.86 = (bf16[256,2048]{1,0:T(8,128)(2,1)}, bf16[256,2048]{1,0:T(8,128)(2,1)}, bf16[256,2048]{1,0:T(8,128)(2,1)}) custom-call(bf16[256,2048]{1,0:T(8,128)(2,1)S(1)} %get-tuple-element.6.a_in, bf16[256,2048]{1,0:T(8,128)(2,1)S(1)} %get-tuple-element.7.b_in, bf16[256,2048]{1,0:T(8,128)(2,1)S(1)} %get-tuple-element.8.c_in), custom_call_target="tpu_custom_call" | custom-call | tf_op jit(solution)/shard_map/pallas_call | solution.py:519

commit v6 on v5

--- a/solution.py
+++ b/solution.py
@@ -130,13 +130,11 @@
     ld = ld_ref[...]
     r_i = lax.broadcasted_iota(jnp.int32, (rows, rows), 0)
     c_i = lax.broadcasted_iota(jnp.int32, (rows, rows), 1)
-    crow[...] = nn(ld, (r_i <= c_i).astype(F32), **exact)
     cum_t = nt((r_i >= c_i).astype(F32), ld, **exact)
     end_t = cum_t[rows - 1:rows, :]
     bg_t = jnp.exp(end_t - cum_t)
     fall_t = jnp.exp(end_t)
     for h in range(heads):
-        cc[h] = jnp.broadcast_to(cum_t[:, h:h + 1], (rows, DH))
         xds[h // piece, h % piece] = jnp.broadcast_to(fall_t[:, h:h + 1], (8, DH))
 
     xd[x] = xds[x]
@@ -188,6 +186,10 @@
             ]
         for u in range(CUTS):
             x_send(0, g * CUTS + u)
+
+    crow[...] = nn(ld, (r_i <= c_i).astype(F32), **exact)
+    for h in range(heads):
+        cc[h] = jnp.broadcast_to(cum_t[:, h:h + 1], (rows, DH))
 
     def z_decays():
         for copy in decay_copies[X_OUT]:

time: 79 us -> 78.6 us (level)
  no operation moved by 1% of the time
where the time goes in v6:
time: 78.6 us; the launch traced here: 78.4 us
  Pallas kernels  77.6 us (99%)
  between operations  0.8 us (1%)
    pallas_call x1, Pallas kernels, shards(): pl.pallas_call(functools.partial(kernel, dims), out_shape=[pltpu.VMEM((ro...  75.8 us
    pallas_call x1, Pallas kernels, shards(): pl.pallas_call(hand_over, out_shape=[jax.ShapeDtypeStruct((rows, width),...  1.76 us

profile of v6, /device:TPU:8, one launch (start us, length us, event | category | flops | bytes accessed | tf_op | source)
XLA Modules:
  0.0 78.4 jit_solution(6764688864713083772)
XLA Ops:
  0.6 75.8 %shard_map.85 = (bf16[256,2048]{1,0:T(8,128)(2,1)S(1)}, bf16[256,2048]{1,0:T(8,128)(2,1)S(1)}, bf16[256,2048]{1,0:T(8,128)(2,1)S(1)}) custom-call(bf16[256,2048]{1,0:T(8,128)(2,1)} %q_in.1, bf16[256,2048]{1,0:T(8,128)(2,1)} %k_in.1, bf16[256,2048]{1,0:T(8,128)(2,1)} %v_in.1, bf16[256,2048]{1,0:T(8,128)(2,1)} %cot_in.1, f32[16,256]{1,0:T(8,128)} %ld_in.1, ...), custom_call_target="tpu_custom_call" | custom-call | tf_op jit(solution)/shard_map/pallas_call | solution.py:508
  76.5 1.8 %shard_map.86 = (bf16[256,2048]{1,0:T(8,128)(2,1)}, bf16[256,2048]{1,0:T(8,128)(2,1)}, bf16[256,2048]{1,0:T(8,128)(2,1)}) custom-call(bf16[256,2048]{1,0:T(8,128)(2,1)S(1)} %get-tuple-element.6.a_in, bf16[256,2048]{1,0:T(8,128)(2,1)S(1)} %get-tuple-element.7.b_in, bf16[256,2048]{1,0:T(8,128)(2,1)S(1)} %get-tuple-element.8.c_in), custom_call_target="tpu_custom_call" | custom-call | tf_op jit(solution)/shard_map/pallas_call | solution.py:521
